TPU v7x, 256 devices: a whole 4x4x8 slice. The times are simulated.
256 devices in a mesh: dp: 64 (over z, y, core), mp: 4 (over x).
Axes of the slice: x: 4, y: 4, z: 8, core: 2. Of those that a mesh axis runs over, the one named last changes fastest.
Arguments:
- query_rows: bfloat16 [16384, 6144], P(('dp', 'mp')), may hold values from -6 to 6
- key_rows: bfloat16 [16384, 6144], P(('dp', 'mp')), may hold values from -6 to 6
- value_rows: bfloat16 [16384, 6144], P(('dp', 'mp')), may hold values from -6 to 6
- destination: int32 [16384], replicated, may hold values from 0 to 63, as said below
- image_slot: int32 [16384], replicated, may hold values from 0 to 5
- gain_query: float32 [48, 128], P('mp'), may hold values from 0.5 to 5
- gain_key: float32 [48, 128], P('mp'), may hold values from 0.5 to 5
- grad_output: bfloat16 [32768, 6144], P('dp', 'mp'), may hold values from -16 to 16
Outputs:
- attention_out: bfloat16 [16384, 6144], P(('dp', 'mp'))
- grad_query: bfloat16 [16384, 6144], P(('dp', 'mp'))
- grad_key: bfloat16 [16384, 6144], P(('dp', 'mp'))
- grad_value: bfloat16 [16384, 6144], P(('dp', 'mp'))
- grad_gain_query: float32 [48, 128], P('mp', 'dp')
- grad_gain_key: float32 [48, 128], P('mp', 'dp')
Inputs may be any that keep to these rules, and one draw needn't show every extreme that they name: `destination`: each loader row's data group. Among the rows of one loader device no group is named more than 2 times, and in every draw some group is named exactly 2 times by the rows of every loader device.
All inputs are finite; a program needn't handle non-finite values.
Results may differ from a plain program's by a relative error of at most 0.005.
The roundings to bfloat16 on the way count: a program that leaves them out, or rounds other values in their place, can miss the bound.
Values may be sent and summed in bfloat16 or wider, within the bound.
A program may use at most 128 MiB of HBM per device.

v0:
```python
import math

import jax
import jax.numpy as jnp
from jax import lax
from jax.sharding import PartitionSpec as P

EPSILON = 1e-06


def normalize(block):
    floats = block.astype(jnp.float32)
    average = jnp.mean(floats, axis=-1, keepdims=True)
    centred = floats - average
    inverse = lax.rsqrt(jnp.mean(centred * centred, axis=-1, keepdims=True) + EPSILON)
    return (centred * inverse, inverse)


def norm_back(grad_hat, normed, inverse):
    first = jnp.mean(grad_hat, axis=-1, keepdims=True)
    second = jnp.mean(grad_hat * normed, axis=-1, keepdims=True)
    return inverse * (grad_hat - first - normed * second)


def head_pass(query_head, key_head, value_head, grad_head, gain_for_query, gain_for_key, allowed):
    query_hat, query_inverse = normalize(query_head)
    key_hat, key_inverse = normalize(key_head)
    query_low = (query_hat * gain_for_query).astype(jnp.bfloat16)
    key_low = (key_hat * gain_for_key).astype(jnp.bfloat16)
    score_scale = 1.0 / math.sqrt(query_head.shape[-1])
    scores = jnp.dot(query_low, key_low.T, preferred_element_type=jnp.float32) * score_scale
    scores = jnp.where(allowed, scores, -1e30)
    row_max = jnp.max(scores, axis=-1, keepdims=True)
    weights = jnp.where(allowed, jnp.exp(scores - row_max), 0.0)
    attention = weights / jnp.sum(weights, axis=-1, keepdims=True)
    attn_low = attention.astype(jnp.bfloat16)
    attn_out = jnp.dot(attn_low, value_head, preferred_element_type=jnp.float32).astype(
        jnp.bfloat16
    )
    grad_probs = jnp.dot(grad_head, value_head.T, preferred_element_type=jnp.float32)
    grad_value = jnp.dot(attn_low.T, grad_head, preferred_element_type=jnp.float32).astype(
        jnp.bfloat16
    )
    row_dot = jnp.sum(attention * grad_probs, axis=-1, keepdims=True)
    grad_scores = (attention * (grad_probs - row_dot) * score_scale).astype(jnp.bfloat16)
    grad_qnorm = jnp.dot(grad_scores, key_low, preferred_element_type=jnp.float32)
    grad_knorm = jnp.dot(grad_scores.T, query_low, preferred_element_type=jnp.float32)
    query_term = jnp.sum(grad_qnorm * query_hat, axis=0)
    key_term = jnp.sum(grad_knorm * key_hat, axis=0)
    grad_query = norm_back(grad_qnorm * gain_for_query, query_hat, query_inverse).astype(
        jnp.bfloat16
    )
    grad_key = norm_back(grad_knorm * gain_for_key, key_hat, key_inverse).astype(jnp.bfloat16)
    return (attn_out, grad_query, grad_key, grad_value, query_term, key_term)


def slot_labels(destination, image_slot, group_id, count_dp, count_mp, capacity):
    sources = count_dp * count_mp
    load_rows = destination.shape[0] // sources
    member = destination.reshape(sources, load_rows) == group_id
    row_rank = jnp.cumsum(member.astype(jnp.int32), axis=1) - 1
    matches = member[:, None, :] & (
        row_rank[:, None, :] == jnp.arange(capacity, dtype=jnp.int32)[None, :, None]
    )
    occupied = jnp.any(matches, axis=-1)
    image_of = jnp.sum(
        jnp.where(matches, image_slot.reshape(sources, load_rows)[:, None, :], 0), axis=-1
    )

    def arrange(label_table):
        return label_table.reshape(count_dp, count_mp, capacity).transpose(1, 0, 2).reshape(-1)

    return (arrange(occupied), arrange(image_of))


def shards(
    query_rows, key_rows, value_rows, destination, image_slot, gain_query, gain_key, grad_output
):
    count_dp = lax.axis_size("dp")
    count_mp = lax.axis_size("mp")
    load_rows = query_rows.shape[0]
    features = query_rows.shape[1]
    head_block = features // count_mp
    local_heads = gain_query.shape[0]
    head_dim = gain_query.shape[1]
    capacity = 2 * load_rows // count_dp
    slot_count = count_mp * count_dp * capacity
    group_id = lax.axis_index("dp")
    source_id = group_id * count_mp + lax.axis_index("mp")
    own_dest = lax.dynamic_slice_in_dim(destination, source_id * load_rows, load_rows)
    member = own_dest[None, :] == jnp.arange(count_dp, dtype=jnp.int32)[:, None]
    row_rank = jnp.cumsum(member.astype(jnp.int32), axis=1) - 1
    matches = member[:, None, :] & (
        row_rank[:, None, :] == jnp.arange(capacity, dtype=jnp.int32)[None, :, None]
    )
    filled = jnp.any(matches, axis=-1).reshape(-1)
    picked = jnp.sum(
        jnp.where(matches, jnp.arange(load_rows, dtype=jnp.int32)[None, None, :], 0), axis=-1
    ).reshape(-1)

    def place_rows(source_rows):
        placed = jnp.take(source_rows, picked, axis=0)
        placed = jnp.where(filled[:, None], placed, jnp.zeros((), source_rows.dtype))
        return placed.reshape(1, count_dp, capacity, count_mp, head_block)

    outgoing = (place_rows(query_rows), place_rows(key_rows), place_rows(value_rows))
    arrived = (
        lax.all_to_all(
            lax.all_to_all(outgoing[0], "dp", split_axis=1, concat_axis=1, tiled=True),
            "mp",
            split_axis=3,
            concat_axis=0,
            tiled=True,
        ),
        lax.all_to_all(
            lax.all_to_all(outgoing[1], "dp", split_axis=1, concat_axis=1, tiled=True),
            "mp",
            split_axis=3,
            concat_axis=0,
            tiled=True,
        ),
        lax.all_to_all(
            lax.all_to_all(outgoing[2], "dp", split_axis=1, concat_axis=1, tiled=True),
            "mp",
            split_axis=3,
            concat_axis=0,
            tiled=True,
        ),
    )

    def by_head(packed):
        return packed.reshape(slot_count, local_heads, head_dim).transpose(1, 0, 2)

    occupied, image_of = slot_labels(
        destination, image_slot, group_id, count_dp, count_mp, capacity
    )
    same_image = image_of[:, None] == image_of[None, :]
    filled_pair = occupied[:, None] & occupied[None, :]
    diagonal_mask = jnp.arange(slot_count)[:, None] == jnp.arange(slot_count)[None, :]
    allowed = filled_pair & same_image | diagonal_mask
    cotangent = jnp.where(occupied[:, None], grad_output, jnp.zeros((), jnp.bfloat16))
    results = lax.map(
        lambda bundle: head_pass(*bundle, allowed),
        (
            by_head(arrived[0]),
            by_head(arrived[1]),
            by_head(arrived[2]),
            by_head(cotangent),
            gain_query,
            gain_key,
        ),
    )

    def to_slots(per_head):
        return per_head.transpose(1, 0, 2).reshape(count_mp, count_dp, capacity, 1, head_block)

    replies = (
        to_slots(results[0]),
        to_slots(results[1]),
        to_slots(results[2]),
        to_slots(results[3]),
    )
    returned = (
        lax.all_to_all(
            lax.all_to_all(replies[0], "dp", split_axis=1, concat_axis=1, tiled=True),
            "mp",
            split_axis=0,
            concat_axis=3,
            tiled=True,
        ),
        lax.all_to_all(
            lax.all_to_all(replies[1], "dp", split_axis=1, concat_axis=1, tiled=True),
            "mp",
            split_axis=0,
            concat_axis=3,
            tiled=True,
        ),
        lax.all_to_all(
            lax.all_to_all(replies[2], "dp", split_axis=1, concat_axis=1, tiled=True),
            "mp",
            split_axis=0,
            concat_axis=3,
            tiled=True,
        ),
        lax.all_to_all(
            lax.all_to_all(replies[3], "dp", split_axis=1, concat_axis=1, tiled=True),
            "mp",
            split_axis=0,
            concat_axis=3,
            tiled=True,
        ),
    )
    own_rank = jnp.sum(jnp.where(member, row_rank, 0), axis=0)
    slot_of_row = own_dest * capacity + own_rank

    def unpack(reply_block):
        return jnp.take(reply_block.reshape(count_dp * capacity, features), slot_of_row, axis=0)

    gain_parts = (
        lax.psum_scatter(results[4], "dp", scatter_dimension=1, tiled=True),
        lax.psum_scatter(results[5], "dp", scatter_dimension=1, tiled=True),
    )
    return (
        unpack(returned[0]),
        unpack(returned[1]),
        unpack(returned[2]),
        unpack(returned[3]),
        gain_parts[0],
        gain_parts[1],
    )


def solution(mesh):
    in_specs = (
        P(("dp", "mp"), None),
        P(("dp", "mp"), None),
        P(("dp", "mp"), None),
        P(),
        P(),
        P("mp", None),
        P("mp", None),
        P("dp", "mp"),
    )
    out_specs = (
        P(("dp", "mp"), None),
        P(("dp", "mp"), None),
        P(("dp", "mp"), None),
        P(("dp", "mp"), None),
        P("mp", "dp"),
        P("mp", "dp"),
    )
    return jax.shard_map(shards, mesh=mesh, in_specs=in_specs, out_specs=out_specs, check_vma=False)
```

profile of v0, /device:TPU:8, one launch (start us, length us, event | category | flops | bytes accessed | tf_op | source)
XLA Modules:
  0.0 997.3 jit_solution(3448278697211551099)
XLA Ops:
  10.5 4.1 select_select_fusion
  20.5 12.1 %all-to-all-start = ((bf16[1,64,2,4,1536]{4,2,3,0,1:T(2,128)(2,1)}), bf16[1,64,2,4,1536]{4,2,3,0,1:T(2,128)(2,1)S(1)}, u32[]{:S(2)}, u32[]{:S(2)}) async-start(bf16[1,64,2,4,1536]{4,2,3,0,1:T(2,128)(2,1)} %copy.107), calls=%async_computation | async-start | bytes 3145728 | tf_op jit(solution)/shard_map/all_to_all | solution.py:109
  34.7 3.8 copy.109
  38.5 34.1 %all-to-all-done = bf16[1,64,2,4,1536]{4,2,3,0,1:T(2,128)(2,1)S(1)} async-done(((bf16[1,64,2,4,1536]{4,2,3,0,1:T(2,128)(2,1)}), bf16[1,64,2,4,1536]{4,2,3,0,1:T(2,128)(2,1)S(1)}, u32[]{:S(2)}, u32[]{:S(2)}) %all-to-all-start) | async-done | bytes 1572896 | tf_op jit(solution)/shard_map/all_to_all | solution.py:109
  72.7 5.8 all-to-all-start.2
  78.4 4.5 reshape.223
  86.8 31.6 %all-to-all-done.2 = bf16[1,64,2,4,1536]{4,2,3,0,1:T(2,128)(2,1)S(1)} async-done(((bf16[1,64,2,4,1536]{4,2,3,0,1:T(2,128)(2,1)}), bf16[1,64,2,4,1536]{4,2,3,0,1:T(2,128)(2,1)S(1)}, u32[]{:S(2)}, u32[]{:S(2)}) %all-to-all-start.2) | async-done | bytes 1572896 | tf_op jit(solution)/shard_map/all_to_all | solution.py:116
  118.3 5.6 all-to-all-start.4
  126.2 37.7 %all-to-all-done.4 = bf16[1,64,2,4,1536]{4,2,3,0,1:T(2,128)(2,1)} async-done(((bf16[1,64,2,4,1536]{4,2,3,0,1:T(2,128)(2,1)}), bf16[1,64,2,4,1536]{4,2,3,0,1:T(2,128)(2,1)}, u32[]{:S(2)}, u32[]{:S(2)}) %all-to-all-start.4) | async-done | bytes 1572896 | tf_op jit(solution)/shard_map/all_to_all | solution.py:123
  163.9 4.3 all-to-all-start.1
  170.4 17.3 %all-to-all-done.1 = bf16[1,64,2,4,1536]{4,2,1,0,3:T(2,128)(2,1)S(1)} async-done(((bf16[1,64,2,4,1536]{4,2,1,0,3:T(2,128)(2,1)}), bf16[1,64,2,4,1536]{4,2,1,0,3:T(2,128)(2,1)S(1)}, u32[]{:S(2)}, u32[]{:S(2)}) %all-to-all-start.1) | async-done | bytes 1572896 | tf_op jit(solution)/shard_map/all_to_all | solution.py:108
  194.9 14.9 %all-to-all-done.3 = bf16[1,64,2,4,1536]{4,2,1,0,3:T(2,128)(2,1)S(1)} async-done(((bf16[1,64,2,4,1536]{4,2,1,0,3:T(2,128)(2,1)}), bf16[1,64,2,4,1536]{4,2,1,0,3:T(2,128)(2,1)S(1)}, u32[]{:S(2)}, u32[]{:S(2)}) %all-to-all-start.3) | async-done | bytes 1572896 | tf_op jit(solution)/shard_map/all_to_all | solution.py:115
  210.9 4.8 all-to-all-start.5
  221.3 4.1 reshape.218
  228.1 4.1 reshape.220
  234.8 4.1 reshape.224
  240.5 221.8 %while.21 = (s32[]{:T(128)}, bf16[12,512,128]{2,1,0:T(8,128)(2,1)}, bf16[12,512,128]{1,2,0:T(8,128)(2,1)}, bf16[12,512,128]{1,2,0:T(8,128)(2,1)}, bf16[12,512,12...) while((s32[]{:T(128)}, bf16[12,512,128]{2,1,0:T(8,128)(2,1)}, ...), condition=%wide.region_20.22_spmd.clone, body=%wide.region_6.21_spmd.clone.sunk | while | flops 421920000 | bytes 13794485 | solution.py:142
  470.2 9.2 all-to-all-start.6
  488.1 31.3 %all-to-all-done.6 = bf16[4,64,2,1,1536]{4,2,0,3,1:T(2,128)(2,1)} async-done(((bf16[4,64,2,1,1536]{4,2,0,3,1:T(2,128)(2,1)}), bf16[4,64,2,1,1536]{4,2,0,3,1:T(2,128)(2,1)}, u32[]{:S(2)}, u32[]{:S(2)}) %all-to-all-start.6) | async-done | bytes 1572896 | tf_op jit(solution)/shard_map/all_to_all | solution.py:165
  519.4 5.6 all-to-all-start.8
  533.6 31.3 %all-to-all-done.8 = bf16[4,64,2,1,1536]{4,2,0,3,1:T(2,128)(2,1)} async-done(((bf16[4,64,2,1,1536]{4,2,0,3,1:T(2,128)(2,1)}), bf16[4,64,2,1,1536]{4,2,0,3,1:T(2,128)(2,1)}, u32[]{:S(2)}, u32[]{:S(2)}) %all-to-all-start.8) | async-done | bytes 1572896 | tf_op jit(solution)/shard_map/all_to_all | solution.py:172
  564.9 6.0 all-to-all-start.10
  578.8 31.9 %all-to-all-done.10 = bf16[4,64,2,1,1536]{4,2,0,3,1:T(2,128)(2,1)} async-done(((bf16[4,64,2,1,1536]{4,2,0,3,1:T(2,128)(2,1)}), bf16[4,64,2,1,1536]{4,2,0,3,1:T(2,128)(2,1)}, u32[]{:S(2)}, u32[]{:S(2)}) %all-to-all-start.10) | async-done | bytes 1572896 | tf_op jit(solution)/shard_map/all_to_all | solution.py:179
  610.7 5.4 all-to-all-start.12
  619.8 36.4 %all-to-all-done.12 = bf16[4,64,2,1,1536]{4,2,0,3,1:T(2,128)(2,1)S(1)} async-done(((bf16[4,64,2,1,1536]{4,2,0,3,1:T(2,128)(2,1)}), bf16[4,64,2,1,1536]{4,2,0,3,1:T(2,128)(2,1)S(1)}, u32[]{:S(2)}, u32[]{:S(2)}) %all-to-all-start.12) | async-done | bytes 1572896 | tf_op jit(solution)/shard_map/all_to_all | solution.py:186
  657.3 4.1 all-to-all-start.7
  665.0 15.9 %all-to-all-done.7 = bf16[4,64,2,1,1536]{4,2,1,3,0:T(2,128)(2,1)S(1)} async-done(((bf16[4,64,2,1,1536]{4,2,1,3,0:T(2,128)(2,1)}), bf16[4,64,2,1,1536]{4,2,1,3,0:T(2,128)(2,1)S(1)}, u32[]{:S(2)}, u32[]{:S(2)}) %all-to-all-start.7) | async-done | bytes 1572896 | tf_op jit(solution)/shard_map/all_to_all | solution.py:164
  688.1 14.9 %all-to-all-done.9 = bf16[4,64,2,1,1536]{4,2,1,3,0:T(2,128)(2,1)S(1)} async-done(((bf16[4,64,2,1,1536]{4,2,1,3,0:T(2,128)(2,1)}), bf16[4,64,2,1,1536]{4,2,1,3,0:T(2,128)(2,1)S(1)}, u32[]{:S(2)}, u32[]{:S(2)}) %all-to-all-start.9) | async-done | bytes 1572896 | tf_op jit(solution)/shard_map/all_to_all | solution.py:171
  703.0 4.3 all-to-all-start.11
  711.0 14.0 %all-to-all-done.11 = bf16[4,64,2,1,1536]{4,2,1,3,0:T(2,128)(2,1)} async-done(((bf16[4,64,2,1,1536]{4,2,1,3,0:T(2,128)(2,1)}), bf16[4,64,2,1,1536]{4,2,1,3,0:T(2,128)(2,1)}, u32[]{:S(2)}, u32[]{:S(2)}) %all-to-all-start.11) | async-done | bytes 1572896 | tf_op jit(solution)/shard_map/all_to_all | solution.py:178
  725.1 4.3 all-to-all-start.13
  731.0 242.3 %all-reduce.2 = (f32[12,128]{0,1:T(8,128)S(1)}, f32[12,128]{0,1:T(8,128)S(1)}) all-reduce(f32[12,128]{0,1:T(8,128)S(1)} %copy.141, f32[12,128]{0,1:T(8,128)S(1)} %copy.142), channel_id=2, replica_groups=mesh['dp'=64,'mp'=4] {'dp'}, use_global_device_ids=true, to_apply=%region_22.25.clone | all-reduce | flops 3072 | bytes 24576
  (402 shorter events, 344.6 us)
Async XLA Ops:
  0.6 1.6 copy-start
  2.3 2.7 copy-start.2
  4.9 2.6 copy-start.3
  20.5 52.1 %all-to-all-start = ((bf16[1,64,2,4,1536]{4,2,3,0,1:T(2,128)(2,1)}), bf16[1,64,2,4,1536]{4,2,3,0,1:T(2,128)(2,1)S(1)}, u32[]{:S(2)}, u32[]{:S(2)}) async-start(bf16[1,64,2,4,1536]{4,2,3,0,1:T(2,128)(2,1)} %copy.107), calls=%async_computation | async-start | bytes 3145728 | tf_op jit(solution)/shard_map/all_to_all | solution.py:109
  72.7 45.7 %all-to-all-start.2 = ((bf16[1,64,2,4,1536]{4,2,3,0,1:T(2,128)(2,1)}), bf16[1,64,2,4,1536]{4,2,3,0,1:T(2,128)(2,1)S(1)}, u32[]{:S(2)}, u32[]{:S(2)}) async-start(bf16[1,64,2,4,1536]{4,2,3,0,1:T(2,128)(2,1)} %copy.109), calls=%async_computation.2 | async-start | bytes 3145728 | tf_op jit(solution)/shard_map/all_to_all | solution.py:116
  118.3 45.6 %all-to-all-start.4 = ((bf16[1,64,2,4,1536]{4,2,3,0,1:T(2,128)(2,1)}), bf16[1,64,2,4,1536]{4,2,3,0,1:T(2,128)(2,1)}, u32[]{:S(2)}, u32[]{:S(2)}) async-start(bf16[1,64,2,4,1536]{4,2,3,0,1:T(2,128)(2,1)} %copy.111), calls=%async_computation.4 | async-start | bytes 3145728 | tf_op jit(solution)/shard_map/all_to_all | solution.py:123
  163.9 23.8 %all-to-all-start.1 = ((bf16[1,64,2,4,1536]{4,2,1,0,3:T(2,128)(2,1)}), bf16[1,64,2,4,1536]{4,2,1,0,3:T(2,128)(2,1)S(1)}, u32[]{:S(2)}, u32[]{:S(2)}) async-start(bf16[1,64,2,4,1536]{4,2,1,0,3:T(2,128)(2,1)} %copy.108), calls=%async_computation.1 | async-start | bytes 3145728 | tf_op jit(solution)/shard_map/all_to_all | solution.py:108
  187.7 22.1 %copy-start.4 = (bf16[1,64,2,4,1536]{4,2,1,0,3:T(2,128)(2,1)}, bf16[1,64,2,4,1536]{4,2,1,0,3:T(2,128)(2,1)S(1)}, u32[]{:S(2)}) copy-start(bf16[1,64,2,4,1536]{4,2,1,0,3:T(2,128)(2,1)S(1)} %all-to-all-done.1) | copy-start | bytes 4718596
  187.7 22.1 %all-to-all-start.3 = ((bf16[1,64,2,4,1536]{4,2,1,0,3:T(2,128)(2,1)}), bf16[1,64,2,4,1536]{4,2,1,0,3:T(2,128)(2,1)S(1)}, u32[]{:S(2)}, u32[]{:S(2)}) async-start(bf16[1,64,2,4,1536]{4,2,1,0,3:T(2,128)(2,1)} %copy.110), calls=%async_computation.3 | async-start | bytes 3145728 | tf_op jit(solution)/shard_map/all_to_all | solution.py:115
  194.9 20.8 %copy-start.9 = (s32[16384]{0:T(1024)S(1)}, s32[16384]{0:T(1024)}, u32[]{:S(2)}) copy-start(s32[16384]{0:T(1024)} %param.17) | copy-start | bytes 196612
  209.8 1.1 copy-start.5
  210.9 23.9 %all-to-all-start.5 = ((bf16[1,64,2,4,1536]{4,2,1,0,3:T(2,128)(2,1)}), bf16[1,64,2,4,1536]{4,2,1,0,3:T(2,128)(2,1)}, u32[]{:S(2)}, u32[]{:S(2)}) async-start(bf16[1,64,2,4,1536]{4,2,1,0,3:T(2,128)(2,1)} %copy.112), calls=%async_computation.5 | async-start | bytes 3145728 | tf_op jit(solution)/shard_map/all_to_all | solution.py:122
  217.2 1.8 copy-start.10
  470.2 49.2 %all-to-all-start.6 = ((bf16[4,64,2,1,1536]{4,2,0,3,1:T(2,128)(2,1)}), bf16[4,64,2,1,1536]{4,2,0,3,1:T(2,128)(2,1)}, u32[]{:S(2)}, u32[]{:S(2)}) async-start(bf16[4,64,2,1,1536]{4,2,0,3,1:T(2,128)(2,1)} %copy.126), calls=%async_computation.6 | async-start | bytes 3145728 | tf_op jit(solution)/shard_map/all_to_all | solution.py:165
  519.4 45.6 %all-to-all-start.8 = ((bf16[4,64,2,1,1536]{4,2,0,3,1:T(2,128)(2,1)}), bf16[4,64,2,1,1536]{4,2,0,3,1:T(2,128)(2,1)}, u32[]{:S(2)}, u32[]{:S(2)}) async-start(bf16[4,64,2,1,1536]{4,2,0,3,1:T(2,128)(2,1)} %copy.130), calls=%async_computation.8 | async-start | bytes 3145728 | tf_op jit(solution)/shard_map/all_to_all | solution.py:172
  564.9 45.8 %all-to-all-start.10 = ((bf16[4,64,2,1,1536]{4,2,0,3,1:T(2,128)(2,1)}), bf16[4,64,2,1,1536]{4,2,0,3,1:T(2,128)(2,1)}, u32[]{:S(2)}, u32[]{:S(2)}) async-start(bf16[4,64,2,1,1536]{4,2,0,3,1:T(2,128)(2,1)} %copy.134), calls=%async_computation.10 | async-start | bytes 3145728 | tf_op jit(solution)/shard_map/all_to_all | solution.py:179
  610.7 45.5 %all-to-all-start.12 = ((bf16[4,64,2,1,1536]{4,2,0,3,1:T(2,128)(2,1)}), bf16[4,64,2,1,1536]{4,2,0,3,1:T(2,128)(2,1)S(1)}, u32[]{:S(2)}, u32[]{:S(2)}) async-start(bf16[4,64,2,1,1536]{4,2,0,3,1:T(2,128)(2,1)} %copy.138), calls=%async_computation.12 | async-start | bytes 3145728 | tf_op jit(solution)/shard_map/all_to_all | solution.py:186
  656.2 1.2 copy-start.6
  657.3 23.6 %all-to-all-start.7 = ((bf16[4,64,2,1,1536]{4,2,1,3,0:T(2,128)(2,1)}), bf16[4,64,2,1,1536]{4,2,1,3,0:T(2,128)(2,1)S(1)}, u32[]{:S(2)}, u32[]{:S(2)}) async-start(bf16[4,64,2,1,1536]{4,2,1,3,0:T(2,128)(2,1)} %copy.127), calls=%async_computation.7 | async-start | bytes 3145728 | tf_op jit(solution)/shard_map/all_to_all | solution.py:164
  680.9 22.1 %all-to-all-start.9 = ((bf16[4,64,2,1,1536]{4,2,1,3,0:T(2,128)(2,1)}), bf16[4,64,2,1,1536]{4,2,1,3,0:T(2,128)(2,1)S(1)}, u32[]{:S(2)}, u32[]{:S(2)}) async-start(bf16[4,64,2,1,1536]{4,2,1,3,0:T(2,128)(2,1)} %copy.131), calls=%async_computation.9 | async-start | bytes 3145728 | tf_op jit(solution)/shard_map/all_to_all | solution.py:171
  703.0 22.1 %all-to-all-start.11 = ((bf16[4,64,2,1,1536]{4,2,1,3,0:T(2,128)(2,1)}), bf16[4,64,2,1,1536]{4,2,1,3,0:T(2,128)(2,1)}, u32[]{:S(2)}, u32[]{:S(2)}) async-start(bf16[4,64,2,1,1536]{4,2,1,3,0:T(2,128)(2,1)} %copy.135), calls=%async_computation.11 | async-start | bytes 3145728 | tf_op jit(solution)/shard_map/all_to_all | solution.py:178
  711.0 18.4 %copy-start.11 = (u32[256]{0:T(256)S(1)}, u32[256]{0:T(256)}, u32[]{:S(2)}) copy-start(u32[256]{0:T(256)} %constant.103) | copy-start | bytes 3076
  725.1 262.9 %all-to-all-start.13 = ((bf16[4,64,2,1,1536]{4,2,1,3,0:T(2,128)(2,1)}), bf16[4,64,2,1,1536]{4,2,1,3,0:T(2,128)(2,1)}, u32[]{:S(2)}, u32[]{:S(2)}) async-start(bf16[4,64,2,1,1536]{4,2,1,3,0:T(2,128)(2,1)} %copy.139), calls=%async_computation.13 | async-start | bytes 3145728 | tf_op jit(solution)/shard_map/all_to_all | solution.py:185
  991.7 1.9 copy-start.7
  991.7 1.9 copy-start.8
  993.6 3.2 copy-start.1
where the time goes:
time: 1010 us; the launch traced here: 997 us
  waiting for transfers between devices  311 us (31%)
  blocking collectives  242 us (24%)
  local copies, waits for them, and re-layouts  141 us (14%)
  matrix products  123 us (12%)
  other arithmetic  98.5 us (10%)
  starting transfers between devices  78.6 us (8%)
    unnamed x1, blocking collectives  242 us
    dynamic_update_slice x24, other arithmetic, shards(): lax.map(lambda bundle: head_pass(*bundle, allowed), (by_head(arrived[0]),...  40.2 us
    all_to_all x1, waiting for transfers between devices, shards(): lax.all_to_all(outgoing[2], 'dp', split_axis=1, concat_axis=1, tiled=True)  37.7 us
    all_to_all x1, waiting for transfers between devices, shards(): lax.all_to_all(replies[3], 'dp', split_axis=1, concat_axis=1, tiled=True)  36.4 us
    all_to_all x1, waiting for transfers between devices, shards(): lax.all_to_all(outgoing[0], 'dp', split_axis=1, concat_axis=1, tiled=True)  34.1 us
    all_to_all x1, waiting for transfers between devices, shards(): lax.all_to_all(replies[2], 'dp', split_axis=1, concat_axis=1, tiled=True)  31.9 us
    all_to_all x1, waiting for transfers between devices, shards(): lax.all_to_all(outgoing[1], 'dp', split_axis=1, concat_axis=1, tiled=True)  31.6 us
    all_to_all x1, waiting for transfers between devices, shards(): lax.all_to_all(replies[1], 'dp', split_axis=1, concat_axis=1, tiled=True)  31.3 us
  transfers between devices with their start and end apart: 14, of which 12 were waited for; matrix products, arithmetic and copies ran while one was open for 10% of the time, Pallas kernels for 0%

commit v1 on v0

v1 whole, which is shorter than its diff:
```python
import functools
import math

import jax
import jax.numpy as jnp
from jax import lax
from jax.experimental import pallas as pl
from jax.experimental.pallas import tpu as pltpu
from jax.sharding import PartitionSpec as P

NZ, NY, NC, NX = 8, 4, 2, 4
POOL = NY * NX
ROWS = 64
WIDE = POOL * ROWS
HD = 128
NH = 3
SLOTS = 512
HALF = SLOTS // NC
PART = HALF // NZ
FEATURES = 6144
EPSILON = 1e-06
MESH = pl.DeviceIdType.MESH
BF = jnp.bfloat16
F32 = jnp.float32
VMEM_LIMIT = 60 * 1024 * 1024


def iota(shape, dim):
    return lax.broadcasted_iota(jnp.int32, shape, dim)


def dot(a, b, ca=1, cb=0):
    return lax.dot_general(a, b, (((ca,), (cb,)), ((), ())), preferred_element_type=F32)


def onehot(flags):
    return jnp.where(flags, 1.0, 0.0).astype(BF)


def coords():
    dp = lax.axis_index("dp")
    return (lax.div(dp, 8), lax.rem(lax.div(dp, 2), 4), lax.rem(dp, 2), lax.axis_index("mp"))


def device(z, y, c, x):
    return ((z * NY + y) * NC + c, x)


def build_tables(cap, z, c, codes, place, expand, lab_col, lab_row, tri):
    lane = iota((1, WIDE), 1)
    lower, upper = iota((WIDE, WIDE), 0), iota((WIDE, WIDE), 1)
    earlier = lower < upper
    tri[...] = onehot(earlier)
    own = codes[pl.ds(z * NC + c, 1), :]
    own_plane = own >> 6
    planes = own_plane == iota((NZ, WIDE), 0)
    mine = jnp.concatenate([codes[pl.ds(u * NC + c, 1), :] for u in range(NZ)], axis=0)
    members = (mine >> 6) == z
    both = jnp.concatenate([onehot(planes), onehot(members)], axis=0)
    before = dot(both, tri[...])
    own_rank = jnp.sum(jnp.where(planes, before[:NZ], 0.0), axis=0, keepdims=True)
    position = own_rank.astype(jnp.int32) + own_plane * cap
    for step in range(NZ):
        place[pl.ds(step * cap, cap), :] = onehot(position == iota((cap, WIDE), 0) + step * cap)
    message_rank = jnp.where(members, before[NZ:], -1.0).astype(jnp.int32)
    tri[...] = onehot(earlier & ((lower >> 6) == (upper >> 6)))
    order = [(jj, cc) for cc in range(NC) for jj in range(NY)]
    source = (lane >> 6) * 2
    for u in range(NZ):
        for k in range(NC):
            core = c if k == 0 else 1 - c
            row = codes[pl.ds(u * NC + core, 1), :]
            group = iota((NZ, WIDE), 0)
            name = z * 8 + (group & 3) * 2 + jnp.where(group < NY, c, 1 - c)
            member = (row >> 3) == name
            count = dot(onehot(member), tri[...])
            slot = jnp.where(member, count + source.astype(F32), -1.0)
            groups = NZ if k == 0 else NY
            blocks = [slot[g : g + 1, :].astype(jnp.int32) == iota((PART, WIDE), 0) for g in range(groups)]
            chosen = onehot(jnp.concatenate(blocks, axis=0))
            image = jnp.broadcast_to(((row & 7) + 1).astype(F32), (HD, WIDE)).astype(BF)
            label = dot(chosen[: NY * PART], image, 1, 1)
            for g in range(NY):
                at = pl.multiple_of(core * HALF + u * PART, PART)
                found = label[g * PART : (g + 1) * PART]
                empty = -1.0 - (at + iota((PART, HD), 0)).astype(F32)
                lab_col[g, pl.ds(at, PART), :] = jnp.where(found > 0.5, found, empty)
            if k == 0:
                ranks = onehot(message_rank[u : u + 1, :] == iota((cap, WIDE), 0))
                expand[u] = dot(chosen, ranks, 1, 1).astype(BF)
    for g in range(NY):
        lab_row[g] = lab_col[g].T[:8]


def normalize(block):
    floats = block.astype(F32)
    average = jnp.mean(floats, axis=-1, keepdims=True)
    centred = floats - average
    inverse = lax.rsqrt(jnp.mean(centred * centred, axis=-1, keepdims=True) + EPSILON)
    return centred * inverse, inverse


def norm_back(grad_hat, normed, inverse):
    first = jnp.mean(grad_hat, axis=-1, keepdims=True)
    second = jnp.mean(grad_hat * normed, axis=-1, keepdims=True)
    return inverse * (grad_hat - first - normed * second)


def head_pass(query, key, value, cot, gain_q, gain_k, col, row, width=256):
    scale = 1.0 / math.sqrt(HD)
    query_hat, query_inverse = normalize(query)
    key_hat, key_inverse = normalize(key)
    query_low = (query_hat * gain_q).astype(BF)
    key_low = (key_hat * gain_k).astype(BF)
    col = jnp.concatenate([col] * (width // HD), axis=1)
    outs, grads_q = [], []
    grad_v = jnp.zeros((SLOTS, HD), F32)
    grad_k = jnp.zeros((SLOTS, HD), F32)
    for at in range(0, SLOTS, width):
        q = query_low[at : at + width]
        g = cot[at : at + width]
        scores = dot(key_low, q, 1, 1)
        scores = jnp.where(col == row[:, at : at + width], scores, -1e30)
        top = jnp.max(scores, axis=0, keepdims=True)
        weights = jnp.exp((scores - top) * scale)
        attention = weights * (1.0 / jnp.sum(weights, axis=0, keepdims=True))
        low = attention.astype(BF)
        probs = dot(value, g, 1, 1)
        inner = jnp.sum(attention * probs, axis=0, keepdims=True)
        grad_s = (attention * (probs - inner) * scale).astype(BF)
        outs.append(dot(low, value, 0, 0))
        grads_q.append(dot(grad_s, key_low, 0, 0))
        grad_v = grad_v + dot(low, g)
        grad_k = grad_k + dot(grad_s, q)
    grad_q = jnp.concatenate(grads_q, axis=0)
    term_q = jnp.sum(grad_q * query_hat, axis=0, keepdims=True)
    term_k = jnp.sum(grad_k * key_hat, axis=0, keepdims=True)
    back_q = norm_back(grad_q * gain_q, query_hat, query_inverse)
    back_k = norm_back(grad_k * gain_k, key_hat, key_inverse)
    packed = jnp.concatenate(
        [jnp.concatenate(outs, axis=0).astype(BF), back_q.astype(BF), back_k.astype(BF), grad_v.astype(BF)],
        axis=1,
    )
    return packed, term_q, term_k


def main_kernel(
    cap, query_in, key_in, value_in, grad_in, gain_q, gain_k, codes, out, gain_out,
    rows, grads, xin, gob, zout, zin, half_out, packed, res, rin, zro, zri,
    place, expand, lab_col, lab_row, tri, shuffle, gacc, gz, gs, gm, gt, gy,
    load_sem, own_sem, grad_own, out_own, xs, xr, gos, gor, zs, zr, hs, hr, rs, rr, zrs, zrr, us, ur,
    gzs, gzr, gms, gmr, gys, gyr,
):
    uout = xin
    z, y, c, x = coords()
    spot = y * NX + x
    loads = [
        pltpu.make_async_copy(ref, rows.at[k], load_sem.at[k])
        for k, ref in enumerate((query_in, key_in, value_in))
    ]
    loads.append(pltpu.make_async_copy(grad_in, grads, load_sem.at[3]))
    for load in loads:
        load.start()

    barrier = pltpu.get_barrier_semaphore()

    def greet(target):
        pl.semaphore_signal(barrier, inc=1, device_id=target, device_id_type=MESH)

    def xy_peer(i):
        return lax.rem(y + lax.div(i, NX), NY), lax.rem(x + lax.rem(i, NX), NX)

    def xy_source(i):
        return lax.rem(y + NY - lax.div(i, NX), NY), lax.rem(x + NX - lax.rem(i, NX), NX)

    def each(low, high, body):
        def step(i, carry):
            body(i)
            return carry

        lax.fori_loop(low, high, step, 0)

    def greet_xy(i):
        py, px = xy_peer(i)
        greet(device(z, py, c, px))

    def greet_z(d):
        greet(device(lax.rem(z + d, NZ), y, c, x))

    each(1, POOL, greet_xy)
    each(1, NZ, greet_z)
    mate = device(z, y, 1 - c, x)
    greet(mate)
    pl.semaphore_wait(barrier, POOL - 1 + NZ - 1 + 1)

    def remote(src, dst, send, recv, target):
        return pltpu.make_async_remote_copy(
            src_ref=src, dst_ref=dst, send_sem=send, recv_sem=recv, device_id=target, device_id_type=MESH
        )

    def columns(py, px, h):
        return pl.ds(pl.multiple_of(px * 1536 + py * 384 + h * HD, HD), HD)

    def xy_copy(h, i):
        py, px = xy_peer(i)
        return remote(
            rows.at[:, :, columns(py, px, h)], xin.at[h, 0:3, spot], xs.at[h, i], xr.at[h, i], device(z, py, c, px)
        )

    def xy_arrival(h, i):
        py, px = xy_source(i)
        return remote(
            rows.at[:, :, columns(y, x, h)], xin.at[h, 0:3, py * NX + px], xs.at[h, i], xr.at[h, i], device(z, py, c, px)
        )

    def xy_own(h):
        return pltpu.make_async_copy(rows.at[:, :, columns(y, x, h)], xin.at[h, 0:3, spot], own_sem.at[h])

    def grad_columns(py, h):
        return pl.ds(pl.multiple_of(py * 384 + h * HD, HD), HD)

    def grad_copy(h, d):
        py = lax.rem(y + d, NY)
        return remote(grads.at[:, grad_columns(py, h)], gob.at[h, y], gos.at[h, d], gor.at[h, d], device(z, py, c, x))

    def grad_arrival(h, d):
        py = lax.rem(y + NY - d, NY)
        return remote(grads.at[:, grad_columns(y, h)], gob.at[h, py], gos.at[h, d], gor.at[h, d], device(z, py, c, x))

    def grad_keep(h):
        return pltpu.make_async_copy(grads.at[:, grad_columns(y, h)], gob.at[h, y], grad_own.at[h])

    for load in loads:
        load.wait()

    def send_rows(h):
        each(1, POOL, lambda i: xy_copy(h, i).start())
        xy_own(h).start()
        each(1, NY, lambda d: grad_copy(h, d).start())
        grad_keep(h).start()

    each(0, NH, send_rows)

    build_tables(cap, z, c, codes, place, expand, lab_col, lab_row, tri)
    slot = iota((SLOTS, SLOTS), 0)
    pool = (slot >> 1) & 15
    canon = (pool & 3) * 128 + ((slot >> 5) & 7) * 16 + (pool >> 2) * 4 + (slot >> 8) * 2 + (slot & 1)
    shuffle[...] = onehot(canon == iota((SLOTS, SLOTS), 1))
    gacc[...] = jnp.zeros_like(gacc)

    def z_copy(h, d):
        pz = lax.rem(z + d, NZ)
        return remote(zout.at[h, pz], zin.at[h, z], zs.at[h, d], zr.at[h, d], device(pz, y, c, x))

    def z_arrival(h, d):
        pz = lax.rem(z + NZ - d, NZ)
        return remote(zout.at[h, pz], zin.at[h, pz], zs.at[h, d], zr.at[h, d], device(pz, y, c, x))

    def message(h, pz):
        pooled = jnp.concatenate([xin[h, k].reshape(WIDE, HD) for k in range(3)], axis=1)
        chosen = place[pl.ds(pl.multiple_of(pz * cap, 16), cap), :]
        return dot(chosen, pooled).astype(BF)

    def compact(h):
        each(1, POOL, lambda i: xy_arrival(h, i).wait_recv())
        xy_own(h).wait()

        def to_plane(d):
            pz = lax.rem(z + d, NZ)
            zout[h, pz] = message(h, pz)
            z_copy(h, d).start()

        each(1, NZ, to_plane)
        zin[h, z] = message(h, z)

    each(0, NH, compact)

    def half_copy(h):
        return remote(half_out.at[h], packed.at[h, :, c], hs.at[h], hr.at[h], mate)

    def half_arrival(h):
        return remote(half_out.at[h], packed.at[h, :, 1 - c], hs.at[h], hr.at[h], mate)

    def res_copy(h):
        return remote(res.at[h, 1 - c], rin.at[h], rs.at[h], rr.at[h], mate)

    def back_copy(h, d):
        pz = lax.rem(z + d, NZ)
        return remote(zro.at[h, pz], zri.at[h, z], zrs.at[h, d], zrr.at[h, d], device(pz, y, c, x))

    def back_arrival(h, d):
        pz = lax.rem(z + NZ - d, NZ)
        return remote(zro.at[h, pz], zri.at[h, pz], zrs.at[h, d], zrr.at[h, d], device(pz, y, c, x))

    def work(h):
        def unfold(pz):
            spread = dot(expand[pz], zin[h, pz]).astype(BF)
            at = pl.ds(pl.multiple_of(pz * PART, PART), PART)
            for g in range(NY):
                packed[h, g, c, at, :] = spread[g * PART : (g + 1) * PART]
                half_out[h, g, at, :] = spread[(NY + g) * PART : (NY + g + 1) * PART]

        unfold(z)

        def arrive(d):
            z_arrival(h, d).wait_recv()
            unfold(lax.rem(z + NZ - d, NZ))

        each(1, NZ, arrive)
        half_copy(h).start()
        each(1, NY, lambda d: grad_arrival(h, d).wait_recv())
        grad_keep(h).wait()
        half_arrival(h).wait_recv()

        head = y * NH + h
        own_gain_q = gain_q[pl.ds(head, 1), :]
        own_gain_k = gain_k[pl.ds(head, 1), :]

        def group(g):
            block = packed[h, g].reshape(SLOTS, 3 * HD)
            col = lab_col[g]
            cot = dot(shuffle[...], gob[h, g])
            cot = jnp.where(col > 0.0, cot, 0.0).astype(BF)
            result, term_q, term_k = head_pass(
                block[:, :HD], block[:, HD : 2 * HD], block[:, 2 * HD :], cot,
                own_gain_q, own_gain_k, col, lab_row[g, 0:1, :],
            )
            res[h, 0, g] = result[:HALF]
            res[h, 1, g] = result[HALF:]
            gacc[h, 0:1, :] += term_q
            gacc[h, 1:2, :] += term_k

        each(0, NY, group)
        res_copy(h).start()
        res_copy(h).wait_recv()

        def fold(pz):
            at = pl.ds(pl.multiple_of(pz * PART, PART), PART)
            blocks = [res[h, c, g, at, :] for g in range(NY)] + [rin[h, g, at, :] for g in range(NY)]
            return dot(expand[pz], jnp.concatenate(blocks, axis=0), 0, 0).astype(BF)

        def send_back(d):
            pz = lax.rem(z + d, NZ)
            zro[h, pz] = fold(pz)
            back_copy(h, d).start()

        each(1, NZ, send_back)
        zri[h, z] = fold(z)

    each(0, NH, work)

    def gz_copy(d):
        return remote(gacc, gz.at[z], gzs.at[d], gzr.at[d], device(lax.rem(z + d, NZ), y, c, x))

    def gz_arrival(d):
        pz = lax.rem(z + NZ - d, NZ)
        return remote(gacc, gz.at[pz], gzs.at[d], gzr.at[d], device(pz, y, c, x))

    def gm_copy():
        return remote(gs, gm, gms, gmr, mate)

    def gy_copy(d):
        return remote(gt, gy.at[y], gys.at[d], gyr.at[d], device(z, lax.rem(y + d, NY), c, x))

    def gy_arrival(d):
        py = lax.rem(y + NY - d, NY)
        return remote(gt, gy.at[py], gys.at[d], gyr.at[d], device(z, py, c, x))

    each(1, NZ, lambda d: gz_copy(d).start())
    gz[z] = gacc[...]

    def u_copy(h, i):
        py, px = xy_peer(i)
        return remote(
            uout.at[h, :, py * NX + px], out.at[:, :, columns(y, x, h)], us.at[h, i], ur.at[h, i], device(z, py, c, px)
        )

    def u_arrival(h, i):
        py, px = xy_source(i)
        return remote(
            uout.at[h, :, spot], out.at[:, :, columns(py, px, h)], us.at[h, i], ur.at[h, i], device(z, py, c, px)
        )

    def u_own(h):
        return pltpu.make_async_copy(uout.at[h, :, spot], out.at[:, :, columns(y, x, h)], out_own.at[h])

    def unpool(h):
        each(1, NZ, lambda d: back_arrival(h, d).wait_recv())

        def block(b):
            chosen = place[:, pl.ds(pl.multiple_of(b * 2 * ROWS, 2 * ROWS), 2 * ROWS)]
            found = dot(chosen, zri[h].reshape(NZ * cap, 4 * HD), 0, 0).astype(BF)
            for k in range(2):
                for a in range(4):
                    uout[h, a, b * 2 + k] = found[k * ROWS : (k + 1) * ROWS, a * HD : (a + 1) * HD]

        each(0, POOL // 2, block)
        each(1, POOL, lambda i: u_copy(h, i).start())
        u_own(h).start()

    unpool(0)
    each(1, NZ, lambda d: gz_arrival(d).wait_recv())
    gs[...] = jnp.sum(gz[...], axis=0)
    gm_copy().start()
    unpool(1)
    gm_copy().wait_recv()
    gt[...] = gs[...] + gm[...]
    each(1, NY, lambda d: gy_copy(d).start())
    gy[y] = gt[...]
    unpool(2)
    each(1, NY, lambda d: gy_arrival(d).wait_recv())
    gain_out[...] = gy[...]

    def finish(h):
        def finish_xy(i):
            u_arrival(h, i).wait_recv()
            u_copy(h, i).wait_send()
            xy_copy(h, i).wait_send()

        each(1, POOL, finish_xy)
        u_own(h).wait()

        def finish_z(d):
            z_copy(h, d).wait_send()
            back_copy(h, d).wait_send()

        each(1, NZ, finish_z)
        each(1, NY, lambda d: grad_copy(h, d).wait_send())
        half_copy(h).wait_send()
        res_copy(h).wait_send()

    each(0, NH, finish)
    each(1, NZ, lambda d: gz_copy(d).wait_send())
    gm_copy().wait_send()
    each(1, NY, lambda d: gy_copy(d).wait_send())


def exchange(cap, collective_id, *operands):
    vmem = pltpu.VMEM
    dma = pltpu.SemaphoreType.DMA
    any_spec = pl.BlockSpec(memory_space=pl.ANY)
    vmem_spec = pl.BlockSpec(memory_space=pltpu.VMEM)
    scratch = [
        vmem((3, ROWS, FEATURES), BF),
        vmem((SLOTS, 1536), BF),
        vmem((NH, 4, POOL, ROWS, HD), BF),
        vmem((NH, NY, SLOTS, HD), BF),
        vmem((NH, NZ, cap, 3 * HD), BF),
        vmem((NH, NZ, cap, 3 * HD), BF),
        vmem((NH, NY, HALF, 3 * HD), BF),
        vmem((NH, NY, NC, HALF, 3 * HD), BF),
        vmem((NH, NC, NY, HALF, 4 * HD), BF),
        vmem((NH, NY, HALF, 4 * HD), BF),
        vmem((NH, NZ, cap, 4 * HD), BF),
        vmem((NH, NZ, cap, 4 * HD), BF),
        vmem((NZ * cap, WIDE), BF),
        vmem((NZ, 2 * NY * PART, cap), BF),
        vmem((NY, SLOTS, HD), F32),
        vmem((NY, 8, SLOTS), F32),
        vmem((WIDE, WIDE), BF),
        vmem((SLOTS, SLOTS), BF),
        vmem((NH, 8, HD), F32),
        vmem((NZ, NH, 8, HD), F32),
        vmem((NH, 8, HD), F32),
        vmem((NH, 8, HD), F32),
        vmem((NH, 8, HD), F32),
        vmem((NY, NH, 8, HD), F32),
        dma((4,)),
        dma((NH,)),
        dma((NH,)),
        dma((NH,)),
    ]
    for width in (POOL, POOL, NY, NY, NZ, NZ):
        scratch.append(dma((NH, width)))
    scratch += [dma((NH,)), dma((NH,)), dma((NH,)), dma((NH,))]
    scratch += [dma((NH, NZ)), dma((NH, NZ)), dma((NH, POOL)), dma((NH, POOL))]
    scratch += [dma((NZ,)), dma((NZ,)), dma(()), dma(()), dma((NY,)), dma((NY,))]
    return pl.pallas_call(
        functools.partial(main_kernel, cap),
        name=f"exchange_{cap}",
        out_shape=(
            jax.ShapeDtypeStruct((4, ROWS, FEATURES), BF),
            jax.ShapeDtypeStruct((NY, NH, 8, HD), F32),
        ),
        in_specs=[any_spec] * 4 + [vmem_spec] * 3,
        out_specs=(any_spec, vmem_spec),
        scratch_shapes=scratch,
        compiler_params=pltpu.CompilerParams(
            collective_id=collective_id, has_side_effects=True, vmem_limit_bytes=VMEM_LIMIT
        ),
    )(*operands)


FULL = POOL * NY * NC * 2


def shards(
    query_rows, key_rows, value_rows, destination, image_slot, gain_query, gain_key, grad_output
):
    codes = (destination * 8 + image_slot).reshape(NZ, NY, NC, NX, ROWS)
    codes = codes.transpose(0, 2, 1, 3, 4).reshape(NZ * NC, WIDE)
    operands = (query_rows, key_rows, value_rows, grad_output, gain_query, gain_key, codes)
    out, gains = exchange(FULL, 0, *operands)
    first = lax.axis_index("dp") * 2
    gains = lax.dynamic_slice_in_dim(gains, first, 2, axis=3)
    grad_gain_query = gains[:, :, 0].reshape(NY * NH, 2)
    grad_gain_key = gains[:, :, 1].reshape(NY * NH, 2)
    return (out[0], out[1], out[2], out[3], grad_gain_query, grad_gain_key)


def solution(mesh):
    in_specs = (
        P(("dp", "mp"), None),
        P(("dp", "mp"), None),
        P(("dp", "mp"), None),
        P(),
        P(),
        P("mp", None),
        P("mp", None),
        P("dp", "mp"),
    )
    out_specs = (
        P(("dp", "mp"), None),
        P(("dp", "mp"), None),
        P(("dp", "mp"), None),
        P(("dp", "mp"), None),
        P("mp", "dp"),
        P("mp", "dp"),
    )
    return jax.shard_map(shards, mesh=mesh, in_specs=in_specs, out_specs=out_specs, check_vma=False)
```

time: 1010 us -> 308 us (0.30); the launches traced: 997 us -> 306 us
  waiting for transfers between devices: 311 us -> 0 us
  Pallas kernels: 0 us -> 297 us
  blocking collectives: 242 us -> 0 us
  local copies, waits for them, and re-layouts: 141 us -> 6.95 us
  matrix products: 123 us -> 0 us
  other arithmetic: 98.5 us -> 0.88 us
  starting transfers between devices: 78.6 us -> 0 us
    all_to_all x14 -> x0, waiting for transfers between devices: 311 us -> none  [the longest x1 37.7 us: shards(): lax.all_to_all(outgoing[2], 'dp', split_axis=1, concat_axis=1, tiled=True)]
    pallas_call x0 -> x1, Pallas kernels: none -> 297 us  [exchange(): pl.pallas_call(functools.partial(main_kernel, cap), name=f'exchange_{cap}...]
    unnamed x1 -> x0, blocking collectives: 242 us -> none
    dot_general x72 -> x0, matrix products: 123 us -> none  [the longest x12 27.4 us: head_pass(): jnp.dot(attn_low, value_head, preferred_element_type=jnp.float32)]
    all_to_all x14 -> x0, starting transfers between devices: 78.6 us -> none  [the longest x1 12.1 us: shards(): lax.all_to_all(outgoing[0], 'dp', split_axis=1, concat_axis=1, tiled=True)]
    reshape x20 -> x2, local copies, waits for them, and re-layouts: 54.1 us -> 0.9 us  [the longest x1 0.78 us: shards(): codes = codes.transpose(0, 2, 1, 3, 4).reshape(NZ * NC, WIDE)]
    reduce_sum x51 -> x0, other arithmetic: 40.7 us -> none  [the longest x24 23.2 us: normalize(): jnp.mean(centred * centred, axis=-1, keepdims=True) + EPSILON]
    dynamic_update_slice x24 -> x0, other arithmetic: 40.2 us -> none  [shards(): lax.map(lambda bundle: head_pass(*bundle, allowed), (by_head(arrived[0]),...]
  transfers between devices with their start and end apart: 14 -> 0, of which waited for: 12 -> 0; matrix products, arithmetic and copies ran while one was open for 10% -> 0% of each run, Pallas kernels for 0% -> 0%
where the time goes in v1:
time: 308 us; the launch traced here: 306 us
  Pallas kernels  297 us (96%)
  local copies, waits for them, and re-layouts  6.95 us (2%)
    pallas_call x1, Pallas kernels, exchange(): pl.pallas_call(functools.partial(main_kernel, cap), name=f'exchange_{cap}...  297 us

profile of v1, /device:TPU:8, one launch (start us, length us, event | category | flops | bytes accessed | tf_op | source)
XLA Modules:
  0.0 306.0 jit_solution(2291729493781830529)
XLA Ops:
  0.6 0.9 multiply_add_fusion
  1.5 0.1 reshape.18
  1.7 0.8 reshape.19.codes
  2.4 297.5 %exchange_256.1 = (bf16[4,64,6144]{2,1,0:T(8,128)(2,1)}, f32[4,3,8,128]{3,2,1,0:T(8,128)}) custom-call(bf16[64,6144]{1,0:T(8,128)(2,1)} %query_in.1, bf16[64,6144]{1,0:T(8,128)(2,1)} %key_in.1, bf16[64,6144]{1,0:T(8,128)(2,1)} %value_in.1, bf16[512,1536]{1,0:T(8,128)(2,1)} %grad_in.1, f32[12,128]{1,0:T(8,128)} %gain_q.1, f32[12,128]{1,0:T(8,128)} %gain_k.1, ...), custom_call_target="tpu_custom_call" | custom-call | tf_op jit(solution)/shard_map/exchange_256/pallas_call | solution.py:478
  299.9 1.0 constant_dynamic-slice_fusion.1
  300.9 0.1 copy.17
  301.0 0.7 reshape_squeeze.6
  301.7 0.1 copy.18
  301.8 0.6 reshape_squeeze.7
  302.4 3.6 %slice_bitcast_fusion = (bf16[64,6144]{1,0:T(8,128)(2,1)}, bf16[64,6144]{1,0:T(8,128)(2,1)}, bf16[64,6144]{1,0:T(8,128)(2,1)}, bf16[64,6144]{1,0:T(8,128)(2,1)}) fusion(bf16[4,64,6144]{2,1,0:T(8,128)(2,1)} %get-tuple-element.8), kind=kLoop, calls=%fused_computation | loop fusion | bytes 6291456 | tf_op jit(solution)/shard_map/squeeze | solution.py:508
  (1 shorter events, 0.0 us)

commit v2 on v1

--- a/solution.py
+++ b/solution.py
@@ -491,7 +491,7 @@
     )(*operands)
 
 
-FULL = POOL * NY * NC * 2
+ROOMS = (160, 176, POOL * NY * NC * 2)
 
 
 def shards(
@@ -500,7 +500,11 @@
     codes = (destination * 8 + image_slot).reshape(NZ, NY, NC, NX, ROWS)
     codes = codes.transpose(0, 2, 1, 3, 4).reshape(NZ * NC, WIDE)
     operands = (query_rows, key_rows, value_rows, grad_output, gain_query, gain_key, codes)
-    out, gains = exchange(FULL, 0, *operands)
+    planes = codes[:, None, :] >> 6 == jnp.arange(NZ, dtype=jnp.int32)[None, :, None]
+    most = jnp.max(jnp.sum(planes.astype(jnp.int32), axis=-1))
+    level = sum((most > room).astype(jnp.int32) for room in ROOMS[:-1])
+    branches = [functools.partial(exchange, room, k) for k, room in enumerate(ROOMS)]
+    out, gains = lax.switch(level, branches, *operands)
     first = lax.axis_index("dp") * 2
     gains = lax.dynamic_slice_in_dim(gains, first, 2, axis=3)
     grad_gain_query = gains[:, :, 0].reshape(NY * NH, 2)

time: 308 us -> 216 us (0.70)
  Pallas kernels: 297 us -> 206 us
    pallas_call x1, Pallas kernels: 297 us -> 206 us  [exchange(): pl.pallas_call(functools.partial(main_kernel, cap), name=f'exchange_{cap}...]
where the time goes in v2:
time: 216 us; the launch traced here: 215 us
  Pallas kernels  206 us (95%)
  local copies, waits for them, and re-layouts  4.25 us (2%)
  between operations  2.19 us (1%)
    pallas_call x1, Pallas kernels, exchange(): pl.pallas_call(functools.partial(main_kernel, cap), name=f'exchange_{cap}...  206 us

profile of v2, /device:TPU:8, one launch (start us, length us, event | category | flops | bytes accessed | tf_op | source)
XLA Modules:
  0.0 214.6 jit_solution(2832800784549191731)
XLA Ops:
  0.6 0.9 multiply_add_fusion
  1.5 0.1 reshape.23
  1.7 0.2 broadcast_in_dim_reshape.3
  1.8 0.4 convert_reduce_fusion
  2.2 0.6 reduce_max.9
  4.1 208.3 %conditional.1 = (f32[4,3,8,128]{3,2,1,0:T(8,128)S(1)}, bf16[64,6144]{1,0:T(8,128)(2,1)S(1)}, bf16[64,6144]{1,0:T(8,128)(2,1)S(1)}, bf16[64,6144]{1,0:T(8,128)(2,1)S(1)}, bf16[64,6144]{1,0:T(8,128)(2,1)S(1)}) conditional(s32[]{:T(128)} %clamp.3, (bf16[64,6144]{1,0:T(8,128)(2,1)}, bf16[64,6144]{1,0:T(8,128)(2,1)}, ...), branch_computations={%region_2.0_spmd.clone.clone, %region_3.0_spmd.clone.clone, %regio... | conditional | bytes 6291496 | solution.py:507
  4.1 206.0 %exchange_160.3 = (bf16[4,64,6144]{2,1,0:T(8,128)(2,1)}, f32[4,3,8,128]{3,2,1,0:T(8,128)S(1)}) custom-call(bf16[64,6144]{1,0:T(8,128)(2,1)} %get-tuple-element.174.query_in, bf16[64,6144]{1,0:T(8,128)(2,1)} %get-tuple-element.175.key_in, bf16[64,6144]{1,0:T(8,128)(2,1)} %get-tuple-element.176.value_in, bf16[512,1536]{1,0:T(8,128)(2,1)} %get-tuple-element.177.grad_in, ...), custom_call_target="tpu_custom_call" | custom-call | tf_op jit(solution)/shard_map/cond/branch_0_fun/exchange_160/pallas_call | solution.py:478
  210.1 2.0 slice_bitcast_fusion
  212.4 0.0 copy-start
  212.4 0.0 copy-start.1
  212.4 0.0 copy-start.2
  212.5 0.0 copy-start.3
  212.5 0.1 constant_dynamic-slice_fusion.1
  212.6 0.1 copy.23
  212.7 0.9 reshape_squeeze.6
  213.6 0.1 copy.24
  213.7 0.6 reshape_squeeze.7
  214.4 0.0 copy-done
  214.4 0.0 copy-done.1
  214.4 0.0 copy-done.2
  214.4 0.0 copy-done.3
  (2 shorter events, 0.0 us)
Async XLA Ops:
  212.4 2.0 copy-start
  212.4 1.9 copy-start.1
  212.4 1.9 copy-start.2
  212.5 1.9 copy-start.3

commit v3 on v2

--- a/solution.py
+++ b/solution.py
@@ -22,6 +22,9 @@
 MESH = pl.DeviceIdType.MESH
 BF = jnp.bfloat16
 F32 = jnp.float32
+OUTWARD = 5
+BACKWARD = 6
+BEHIND = 3
 VMEM_LIMIT = 60 * 1024 * 1024
 
 
@@ -46,8 +49,7 @@
     return ((z * NY + y) * NC + c, x)
 
 
-def build_tables(cap, z, c, codes, place, expand, lab_col, lab_row, tri):
-    lane = iota((1, WIDE), 1)
+def build_place(cap, z, c, codes, place, tri):
     lower, upper = iota((WIDE, WIDE), 0), iota((WIDE, WIDE), 1)
     earlier = lower < upper
     tri[...] = onehot(earlier)
@@ -62,9 +64,17 @@
     position = own_rank.astype(jnp.int32) + own_plane * cap
     for step in range(NZ):
         place[pl.ds(step * cap, cap), :] = onehot(position == iota((cap, WIDE), 0) + step * cap)
-    message_rank = jnp.where(members, before[NZ:], -1.0).astype(jnp.int32)
+    return position, jnp.where(members, before[NZ:], -1.0).astype(jnp.int32)
+
+
+def build_expand(cap, z, c, position, message_rank, codes, turned, expand, lab_col, lab_row, tri):
+    column = jnp.broadcast_to(position.astype(F32), (HD, WIDE)).T
+    for k in range(0, NZ * cap, HD):
+        turned[:, k : k + HD] = onehot(column == (iota((WIDE, HD), 1) + k).astype(F32))
+    lane = iota((1, WIDE), 1)
+    lower, upper = iota((WIDE, WIDE), 0), iota((WIDE, WIDE), 1)
+    earlier = lower < upper
     tri[...] = onehot(earlier & ((lower >> 6) == (upper >> 6)))
-    order = [(jj, cc) for cc in range(NC) for jj in range(NY)]
     source = (lane >> 6) * 2
     for u in range(NZ):
         for k in range(NC):
@@ -146,12 +156,13 @@
 
 def main_kernel(
     cap, query_in, key_in, value_in, grad_in, gain_q, gain_k, codes, out, gain_out,
-    rows, grads, xin, gob, zout, zin, half_out, packed, res, rin, zro, zri,
-    place, expand, lab_col, lab_row, tri, shuffle, gacc, gz, gs, gm, gt, gy,
+    rows, grads, xin, gob, zin, half_out, packed, res, rin, zro, zri,
+    place, turned, expand, lab_col, lab_row, tri, shuffle, gacc, gz, gs, gm, gt, gy,
     load_sem, own_sem, grad_own, out_own, xs, xr, gos, gor, zs, zr, hs, hr, rs, rr, zrs, zrr, us, ur,
     gzs, gzr, gms, gmr, gys, gyr,
 ):
     uout = xin
+    zout = zro
     z, y, c, x = coords()
     spot = y * NX + x
     loads = [
@@ -170,9 +181,6 @@
     def xy_peer(i):
         return lax.rem(y + lax.div(i, NX), NY), lax.rem(x + lax.rem(i, NX), NX)
 
-    def xy_source(i):
-        return lax.rem(y + NY - lax.div(i, NX), NY), lax.rem(x + NX - lax.rem(i, NX), NX)
-
     def each(low, high, body):
         def step(i, carry):
             body(i)
@@ -201,20 +209,35 @@
     def columns(py, px, h):
         return pl.ds(pl.multiple_of(px * 1536 + py * 384 + h * HD, HD), HD)
 
-    def xy_copy(h, i):
-        py, px = xy_peer(i)
-        return remote(
-            rows.at[:, :, columns(py, px, h)], xin.at[h, 0:3, spot], xs.at[h, i], xr.at[h, i], device(z, py, c, px)
+    def piece(h, a):
+        return a if isinstance(h, int) and h == 0 else h + 2
+
+    def xy_start(h, a, n):
+        f = piece(h, a)
+
+        def start(i):
+            py, px = xy_peer(i)
+            remote(
+                rows.at[pl.ds(a, n), :, columns(py, px, h)], xin.at[h, pl.ds(a, n), spot],
+                xs.at[f], xr.at[f], device(z, py, c, px),
+            ).start()
+
+        each(1, POOL, start)
+        xy_own(h, a, n).start()
+
+    def xy_own(h, a, n):
+        return pltpu.make_async_copy(
+            rows.at[pl.ds(a, n), :, columns(y, x, h)], xin.at[h, pl.ds(a, n), spot], own_sem.at[piece(h, a)]
         )
 
-    def xy_arrival(h, i):
-        py, px = xy_source(i)
-        return remote(
-            rows.at[:, :, columns(y, x, h)], xin.at[h, 0:3, py * NX + px], xs.at[h, i], xr.at[h, i], device(z, py, c, px)
-        )
-
-    def xy_own(h):
-        return pltpu.make_async_copy(rows.at[:, :, columns(y, x, h)], xin.at[h, 0:3, spot], own_sem.at[h])
+    def xy_all(h, a, n):
+        f = piece(h, a)
+        area = xin.at[h, pl.ds(a, n), 0 : POOL - 1]
+        return remote(area, area, xs.at[f], xr.at[f], mate)
+
+    def xy_arrive(h, a, n):
+        xy_all(h, a, n).wait_recv()
+        xy_own(h, a, n).wait()
 
     def grad_columns(py, h):
         return pl.ds(pl.multiple_of(py * 384 + h * HD, HD), HD)
@@ -230,83 +253,105 @@
     def grad_keep(h):
         return pltpu.make_async_copy(grads.at[:, grad_columns(y, h)], gob.at[h, y], grad_own.at[h])
 
-    for load in loads:
-        load.wait()
-
-    def send_rows(h):
-        each(1, POOL, lambda i: xy_copy(h, i).start())
-        xy_own(h).start()
+    def send_grads(h):
         each(1, NY, lambda d: grad_copy(h, d).start())
         grad_keep(h).start()
 
-    each(0, NH, send_rows)
-
-    build_tables(cap, z, c, codes, place, expand, lab_col, lab_row, tri)
+    for k in range(3):
+        loads[k].wait()
+        xy_start(0, k, 1)
+    loads[3].wait()
+    position, message_rank = build_place(cap, z, c, codes, place, tri)
     slot = iota((SLOTS, SLOTS), 0)
     pool = (slot >> 1) & 15
     canon = (pool & 3) * 128 + ((slot >> 5) & 7) * 16 + (pool >> 2) * 4 + (slot >> 8) * 2 + (slot & 1)
     shuffle[...] = onehot(canon == iota((SLOTS, SLOTS), 1))
     gacc[...] = jnp.zeros_like(gacc)
 
-    def z_copy(h, d):
-        pz = lax.rem(z + d, NZ)
-        return remote(zout.at[h, pz], zin.at[h, z], zs.at[h, d], zr.at[h, d], device(pz, y, c, x))
+    def z_all(h):
+        area = zout.at[h, 0 : NZ - 1, :, 0 : 3 * HD]
+        return remote(area, area, zs.at[h], zr.at[h, 0], mate)
 
     def z_arrival(h, d):
-        pz = lax.rem(z + NZ - d, NZ)
-        return remote(zout.at[h, pz], zin.at[h, pz], zs.at[h, d], zr.at[h, d], device(pz, y, c, x))
-
-    def message(h, pz):
-        pooled = jnp.concatenate([xin[h, k].reshape(WIDE, HD) for k in range(3)], axis=1)
-        chosen = place[pl.ds(pl.multiple_of(pz * cap, 16), cap), :]
-        return dot(chosen, pooled).astype(BF)
-
-    def compact(h):
-        each(1, POOL, lambda i: xy_arrival(h, i).wait_recv())
-        xy_own(h).wait()
+        area = zin.at[h, lax.rem(z + NZ - d, NZ)]
+        return remote(area, area, zs.at[h], zr.at[h, d], mate)
+
+    def compact(h, a, n):
+        part = slice(a * HD, (a + n) * HD)
+
+        def message(pz):
+            if n == 1:
+                pooled = xin[h, a].reshape(WIDE, HD)
+            else:
+                pooled = jnp.concatenate([xin[h, k].reshape(WIDE, HD) for k in range(n)], axis=1)
+            chosen = place[pl.ds(pl.multiple_of(pz * cap, 16), cap), :]
+            return dot(chosen, pooled).astype(BF)
 
         def to_plane(d):
             pz = lax.rem(z + d, NZ)
-            zout[h, pz] = message(h, pz)
-            z_copy(h, d).start()
-
-        each(1, NZ, to_plane)
-        zin[h, z] = message(h, z)
-
-    each(0, NH, compact)
+            found = message(pz)
+
+            @pl.when(d < NZ)
+            def _():
+                zout[h, pz, :, part] = found
+                remote(
+                    zout.at[h, pz, :, part], zin.at[h, z, :, part], zs.at[h], zr.at[h, d], device(pz, y, c, x)
+                ).start()
+
+            @pl.when(d == NZ)
+            def _():
+                zin[h, z, :, part] = found
+
+        each(1, NZ + 1, to_plane)
+
+    def first_head(a):
+        xy_arrive(0, a, 1)
+        if a == 1:
+            xy_start(1, 0, 3)
+        if a == 2:
+            send_grads(0)
+        compact(0, a, 1)
+
+    for a in range(3):
+        first_head(a)
+    build_expand(cap, z, c, position, message_rank, codes, turned, expand, lab_col, lab_row, tri)
+
+    def other_head(h):
+        xy_arrive(h, 0, 3)
+
+        @pl.when(h == 1)
+        def _():
+            xy_start(2, 0, 3)
+
+        send_grads(h)
+        compact(h, 0, 3)
+
+    each(1, NH, other_head)
 
     def half_copy(h):
-        return remote(half_out.at[h], packed.at[h, :, c], hs.at[h], hr.at[h], mate)
+        return remote(half_out, packed.at[h, :, c], hs.at[h], hr.at[h], mate)
 
     def half_arrival(h):
-        return remote(half_out.at[h], packed.at[h, :, 1 - c], hs.at[h], hr.at[h], mate)
+        return remote(half_out, packed.at[h, :, 1 - c], hs.at[h], hr.at[h], mate)
 
     def res_copy(h):
-        return remote(res.at[h, 1 - c], rin.at[h], rs.at[h], rr.at[h], mate)
-
-    def back_copy(h, d):
-        pz = lax.rem(z + d, NZ)
-        return remote(zro.at[h, pz], zri.at[h, z], zrs.at[h, d], zrr.at[h, d], device(pz, y, c, x))
-
-    def back_arrival(h, d):
-        pz = lax.rem(z + NZ - d, NZ)
-        return remote(zro.at[h, pz], zri.at[h, pz], zrs.at[h, d], zrr.at[h, d], device(pz, y, c, x))
+        return remote(res.at[1 - c], rin, rs.at[h], rr.at[h], mate)
 
     def work(h):
-        def unfold(pz):
+        def unfold(d):
+            pz = lax.rem(z + NZ - d, NZ)
+
+            @pl.when(d > 0)
+            def _():
+                z_arrival(h, d).wait_recv()
+
             spread = dot(expand[pz], zin[h, pz]).astype(BF)
             at = pl.ds(pl.multiple_of(pz * PART, PART), PART)
             for g in range(NY):
                 packed[h, g, c, at, :] = spread[g * PART : (g + 1) * PART]
-                half_out[h, g, at, :] = spread[(NY + g) * PART : (NY + g + 1) * PART]
-
-        unfold(z)
-
-        def arrive(d):
-            z_arrival(h, d).wait_recv()
-            unfold(lax.rem(z + NZ - d, NZ))
-
-        each(1, NZ, arrive)
+                half_out[g, at, :] = spread[(NY + g) * PART : (NY + g + 1) * PART]
+
+        each(0, NZ, unfold)
         half_copy(h).start()
         each(1, NY, lambda d: grad_arrival(h, d).wait_recv())
         grad_keep(h).wait()
@@ -325,29 +370,78 @@
                 block[:, :HD], block[:, HD : 2 * HD], block[:, 2 * HD :], cot,
                 own_gain_q, own_gain_k, col, lab_row[g, 0:1, :],
             )
-            res[h, 0, g] = result[:HALF]
-            res[h, 1, g] = result[HALF:]
+            res[0, g] = result[:HALF]
+            res[1, g] = result[HALF:]
             gacc[h, 0:1, :] += term_q
             gacc[h, 1:2, :] += term_k
 
         each(0, NY, group)
         res_copy(h).start()
-        res_copy(h).wait_recv()
-
-        def fold(pz):
+        res_copy(h).wait()
+        half_copy(h).wait_send()
+        z_all(h).wait_send()
+
+    def back_all(b):
+        area = zri.at[0, 0 : NZ - 1, :, 0 : 2 * HD]
+        return remote(area, area, zrs.at[b], zrr.at[b], mate)
+
+    def send_back(h, half):
+        b = h * 2 + half
+        part = slice(half * 2 * HD, (half + 1) * 2 * HD)
+
+        def fold(d):
+            pz = lax.rem(z + d, NZ)
             at = pl.ds(pl.multiple_of(pz * PART, PART), PART)
-            blocks = [res[h, c, g, at, :] for g in range(NY)] + [rin[h, g, at, :] for g in range(NY)]
-            return dot(expand[pz], jnp.concatenate(blocks, axis=0), 0, 0).astype(BF)
-
-        def send_back(d):
-            pz = lax.rem(z + d, NZ)
-            zro[h, pz] = fold(pz)
-            back_copy(h, d).start()
-
-        each(1, NZ, send_back)
-        zri[h, z] = fold(z)
-
-    each(0, NH, work)
+            blocks = [res[c, g, at, part] for g in range(NY)] + [rin[g, at, part] for g in range(NY)]
+            folded = dot(expand[pz], jnp.concatenate(blocks, axis=0), 0, 0).astype(BF)
+
+            @pl.when(d < NZ)
+            def _():
+                zro[h, pz, :, part] = folded
+                remote(
+                    zro.at[h, pz, :, part], zri.at[h, z, :, part], zrs.at[b], zrr.at[b], device(pz, y, c, x)
+                ).start()
+
+            @pl.when(d == NZ)
+            def _():
+                zri[h, z, :, part] = folded
+
+        each(1, NZ + 1, fold)
+
+    def u_own(b):
+        h = lax.div(b, 2)
+        two = pl.ds(lax.rem(b, 2) * 2, 2)
+        return pltpu.make_async_copy(uout.at[h, two, spot], out.at[two, :, columns(y, x, h)], out_own.at[b])
+
+    def u_all(b):
+        area = out.at[0:2, :, 0 : (POOL - 1) * HD]
+        return remote(area, area, us.at[b], ur.at[b], mate)
+
+    def unpool(h, half):
+        b = h * 2 + half
+        first = half * 2
+        part = slice(first * HD, (first + 2) * HD)
+        back_all(b).wait_recv()
+
+        def block(k):
+            chosen = turned[pl.ds(pl.multiple_of(k * 4 * ROWS, 4 * ROWS), 4 * ROWS), :]
+            found = dot(chosen, zri[h, :, :, part].reshape(NZ * cap, 2 * HD)).astype(BF)
+            for r in range(4):
+                for m in range(2):
+                    uout[h, first + m, k * 4 + r] = found[r * ROWS : (r + 1) * ROWS, m * HD : (m + 1) * HD]
+
+        each(0, POOL // 4, block)
+
+        def start(i):
+            py, px = xy_peer(i)
+            two = pl.ds(first, 2)
+            remote(
+                uout.at[h, two, py * NX + px], out.at[two, :, columns(y, x, h)],
+                us.at[b], ur.at[b], device(z, py, c, px),
+            ).start()
+
+        each(1, POOL, start)
+        u_own(b).start()
 
     def gz_copy(d):
         return remote(gacc, gz.at[z], gzs.at[d], gzr.at[d], device(lax.rem(z + d, NZ), y, c, x))
@@ -366,73 +460,68 @@
         py = lax.rem(y + NY - d, NY)
         return remote(gt, gy.at[py], gys.at[d], gyr.at[d], device(z, py, c, x))
 
-    each(1, NZ, lambda d: gz_copy(d).start())
-    gz[z] = gacc[...]
-
-    def u_copy(h, i):
-        py, px = xy_peer(i)
-        return remote(
-            uout.at[h, :, py * NX + px], out.at[:, :, columns(y, x, h)], us.at[h, i], ur.at[h, i], device(z, py, c, px)
-        )
-
-    def u_arrival(h, i):
-        py, px = xy_source(i)
-        return remote(
-            uout.at[h, :, spot], out.at[:, :, columns(py, px, h)], us.at[h, i], ur.at[h, i], device(z, py, c, px)
-        )
-
-    def u_own(h):
-        return pltpu.make_async_copy(uout.at[h, :, spot], out.at[:, :, columns(y, x, h)], out_own.at[h])
-
-    def unpool(h):
-        each(1, NZ, lambda d: back_arrival(h, d).wait_recv())
-
-        def block(b):
-            chosen = place[:, pl.ds(pl.multiple_of(b * 2 * ROWS, 2 * ROWS), 2 * ROWS)]
-            found = dot(chosen, zri[h].reshape(NZ * cap, 4 * HD), 0, 0).astype(BF)
-            for k in range(2):
-                for a in range(4):
-                    uout[h, a, b * 2 + k] = found[k * ROWS : (k + 1) * ROWS, a * HD : (a + 1) * HD]
-
-        each(0, POOL // 2, block)
-        each(1, POOL, lambda i: u_copy(h, i).start())
-        u_own(h).start()
-
-    unpool(0)
-    each(1, NZ, lambda d: gz_arrival(d).wait_recv())
-    gs[...] = jnp.sum(gz[...], axis=0)
-    gm_copy().start()
-    unpool(1)
-    gm_copy().wait_recv()
-    gt[...] = gs[...] + gm[...]
-    each(1, NY, lambda d: gy_copy(d).start())
-    gy[y] = gt[...]
-    unpool(2)
-    each(1, NY, lambda d: gy_arrival(d).wait_recv())
-    gain_out[...] = gy[...]
-
-    def finish(h):
-        def finish_xy(i):
-            u_arrival(h, i).wait_recv()
-            u_copy(h, i).wait_send()
-            xy_copy(h, i).wait_send()
-
-        each(1, POOL, finish_xy)
-        u_own(h).wait()
-
-        def finish_z(d):
-            z_copy(h, d).wait_send()
-            back_copy(h, d).wait_send()
-
-        each(1, NZ, finish_z)
-        each(1, NY, lambda d: grad_copy(h, d).wait_send())
-        half_copy(h).wait_send()
-        res_copy(h).wait_send()
-
-    each(0, NH, finish)
-    each(1, NZ, lambda d: gz_copy(d).wait_send())
-    gm_copy().wait_send()
-    each(1, NY, lambda d: gy_copy(d).wait_send())
+    def back(h, half):
+        b = h * 2 + half
+        if half == 0:
+
+            @pl.when(b < BACKWARD)
+            def _():
+                work(h)
+
+        @pl.when((b >= BEHIND) & (b < BACKWARD + BEHIND))
+        def _():
+            back_all(b - BEHIND).wait_send()
+
+        @pl.when(b < BACKWARD)
+        def _():
+            send_back(h, half)
+
+        @pl.when(b == BACKWARD - 1)
+        def _():
+            each(1, NZ, lambda d: gz_copy(d).start())
+            gz[z] = gacc[...]
+
+        @pl.when(b == BACKWARD)
+        def _():
+            each(1, NZ, lambda d: gz_arrival(d).wait_recv())
+            gs[...] = jnp.sum(gz[...], axis=0)
+            gm_copy().start()
+            for f in range(3):
+                xy_all(0, f, 1).wait_send()
+            for h in range(1, NH):
+                xy_all(h, 0, 3).wait_send()
+            each(0, NH, lambda h: each(1, NY, lambda d: grad_copy(h, d).wait_send()))
+
+        @pl.when(b == BACKWARD + 1)
+        def _():
+            gm_copy().wait_recv()
+            gt[...] = gs[...] + gm[...]
+            each(1, NY, lambda d: gy_copy(d).start())
+            gy[y] = gt[...]
+
+        @pl.when(b == BACKWARD + 2)
+        def _():
+            each(1, NY, lambda d: gy_arrival(d).wait_recv())
+            gain_out[...] = gy[...]
+            each(1, NZ, lambda d: gz_copy(d).wait_send())
+            gm_copy().wait_send()
+            each(1, NY, lambda d: gy_copy(d).wait_send())
+
+        @pl.when((b >= BEHIND) & (b < BACKWARD + BEHIND))
+        def _():
+            unpool(h + (half - BEHIND) // 2, (half - BEHIND) % 2)
+
+    def both(h):
+        for half in range(2):
+            back(h, half)
+
+    each(0, (BACKWARD + BEHIND + 1) // 2, both)
+
+    def finish(b):
+        u_all(b).wait()
+        u_own(b).wait()
+
+    each(0, BACKWARD, finish)
 
 
 def exchange(cap, collective_id, *operands):
@@ -446,14 +535,14 @@
         vmem((NH, 4, POOL, ROWS, HD), BF),
         vmem((NH, NY, SLOTS, HD), BF),
         vmem((NH, NZ, cap, 3 * HD), BF),
-        vmem((NH, NZ, cap, 3 * HD), BF),
-        vmem((NH, NY, HALF, 3 * HD), BF),
+        vmem((NY, HALF, 3 * HD), BF),
         vmem((NH, NY, NC, HALF, 3 * HD), BF),
-        vmem((NH, NC, NY, HALF, 4 * HD), BF),
-        vmem((NH, NY, HALF, 4 * HD), BF),
+        vmem((NC, NY, HALF, 4 * HD), BF),
+        vmem((NY, HALF, 4 * HD), BF),
         vmem((NH, NZ, cap, 4 * HD), BF),
         vmem((NH, NZ, cap, 4 * HD), BF),
         vmem((NZ * cap, WIDE), BF),
+        vmem((WIDE, NZ * cap), BF),
         vmem((NZ, 2 * NY * PART, cap), BF),
         vmem((NY, SLOTS, HD), F32),
         vmem((NY, 8, SLOTS), F32),
@@ -466,14 +555,18 @@
         vmem((NH, 8, HD), F32),
         vmem((NY, NH, 8, HD), F32),
         dma((4,)),
+        dma((OUTWARD,)),
         dma((NH,)),
+        dma((BACKWARD,)),
+        dma((OUTWARD,)),
+        dma((OUTWARD,)),
+        dma((NH, NY)),
+        dma((NH, NY)),
         dma((NH,)),
-        dma((NH,)),
+        dma((NH, NZ)),
     ]
-    for width in (POOL, POOL, NY, NY, NZ, NZ):
-        scratch.append(dma((NH, width)))
     scratch += [dma((NH,)), dma((NH,)), dma((NH,)), dma((NH,))]
-    scratch += [dma((NH, NZ)), dma((NH, NZ)), dma((NH, POOL)), dma((NH, POOL))]
+    scratch += [dma((BACKWARD,)), dma((BACKWARD,)), dma((BACKWARD,)), dma((BACKWARD,))]
     scratch += [dma((NZ,)), dma((NZ,)), dma(()), dma(()), dma((NY,)), dma((NY,))]
     return pl.pallas_call(
         functools.partial(main_kernel, cap),

time: 216 us -> 199 us (0.921)
  Pallas kernels: 206 us -> 190 us
    pallas_call x1, Pallas kernels: 206 us -> 190 us  [exchange(): pl.pallas_call(functools.partial(main_kernel, cap), name=f'exchange_{cap}...]
where the time goes in v3:
time: 199 us; the launch traced here: 198 us
  Pallas kernels  190 us (95%)
  local copies, waits for them, and re-layouts  4.22 us (2%)
  between operations  2.23 us (1%)
    pallas_call x1, Pallas kernels, exchange(): pl.pallas_call(functools.partial(main_kernel, cap), name=f'exchange_{cap}...  190 us

profile of v3, /device:TPU:8, one launch (start us, length us, event | category | flops | bytes accessed | tf_op | source)
XLA Modules:
  0.0 198.5 jit_solution(13187855873011035449)
XLA Ops:
  0.6 0.9 multiply_add_fusion
  1.5 0.1 reshape.23
  1.7 0.2 broadcast_in_dim_reshape.3
  1.8 0.4 convert_reduce_fusion
  2.2 0.6 reduce_max.9
  4.1 192.2 %conditional.1 = (f32[4,3,8,128]{3,2,1,0:T(8,128)S(1)}, bf16[64,6144]{1,0:T(8,128)(2,1)S(1)}, bf16[64,6144]{1,0:T(8,128)(2,1)S(1)}, bf16[64,6144]{1,0:T(8,128)(2,1)S(1)}, bf16[64,6144]{1,0:T(8,128)(2,1)S(1)}) conditional(s32[]{:T(128)} %clamp.3, (bf16[64,6144]{1,0:T(8,128)(2,1)}, bf16[64,6144]{1,0:T(8,128)(2,1)}, ...), branch_computations={%region_2.0_spmd.clone.clone, %region_3.0_spmd.clone.clone, %regio... | conditional | bytes 6291496 | solution.py:600
  4.1 189.6 %exchange_160.3 = (bf16[4,64,6144]{2,1,0:T(8,128)(2,1)}, f32[4,3,8,128]{3,2,1,0:T(8,128)S(1)}) custom-call(bf16[64,6144]{1,0:T(8,128)(2,1)} %get-tuple-element.174.query_in, bf16[64,6144]{1,0:T(8,128)(2,1)} %get-tuple-element.175.key_in, bf16[64,6144]{1,0:T(8,128)(2,1)} %get-tuple-element.176.value_in, bf16[512,1536]{1,0:T(8,128)(2,1)} %get-tuple-element.177.grad_in, ...), custom_call_target="tpu_custom_call" | custom-call | tf_op jit(solution)/shard_map/cond/branch_0_fun/exchange_160/pallas_call | solution.py:571
  193.7 2.0 %slice_bitcast_fusion = (bf16[64,6144]{1,0:T(8,128)(2,1)S(1)}, bf16[64,6144]{1,0:T(8,128)(2,1)S(1)}, bf16[64,6144]{1,0:T(8,128)(2,1)S(1)}, bf16[64,6144]{1,0:T(8,128)(2,1)S(1)}) fusion(bf16[4,64,6144]{2,1,0:T(8,128)(2,1)} %get-tuple-element.181), kind=kLoop, calls=%fused_computation | loop fusion | bytes 6291456 | tf_op jit(solution)/shard_map/squeeze | solution.py:605
  196.3 0.0 copy-start
  196.3 0.0 copy-start.1
  196.3 0.0 copy-start.2
  196.3 0.0 copy-start.3
  196.4 0.1 constant_dynamic-slice_fusion.1
  196.5 0.1 copy.23
  196.6 0.9 reshape_squeeze.6
  197.5 0.1 copy.24
  197.6 0.6 reshape_squeeze.7
  198.2 0.0 copy-done
  198.2 0.0 copy-done.1
  198.2 0.0 copy-done.2
  198.2 0.0 copy-done.3
  (2 shorter events, 0.0 us)
Async XLA Ops:
  196.3 1.9 copy-start
  196.3 1.9 copy-start.1
  196.3 1.9 copy-start.2
  196.3 1.9 copy-start.3

commit v4 on v3

--- a/solution.py
+++ b/solution.py
@@ -24,7 +24,7 @@
 F32 = jnp.float32
 OUTWARD = 5
 BACKWARD = 6
-BEHIND = 3
+BEHIND = 2
 VMEM_LIMIT = 60 * 1024 * 1024
 
 
@@ -515,7 +515,7 @@
         for half in range(2):
             back(h, half)
 
-    each(0, (BACKWARD + BEHIND + 1) // 2, both)
+    each(0, 5, both)
 
     def finish(b):
         u_all(b).wait()

time: 199 us -> 193 us (0.970)
  Pallas kernels: 190 us -> 184 us
    pallas_call x1, Pallas kernels: 190 us -> 184 us  [exchange(): pl.pallas_call(functools.partial(main_kernel, cap), name=f'exchange_{cap}...]
where the time goes in v4:
time: 193 us
  Pallas kernels  184 us (95%)
  local copies, waits for them, and re-layouts  4.22 us (2%)
  between operations  2.23 us (1%)
    pallas_call x1, Pallas kernels, exchange(): pl.pallas_call(functools.partial(main_kernel, cap), name=f'exchange_{cap}...  184 us

profile of v4, /device:TPU:8, one launch (start us, length us, event | category | flops | bytes accessed | tf_op | source)
XLA Modules:
  0.0 192.8 jit_solution(6527940229550392370)
XLA Ops:
  0.6 0.9 multiply_add_fusion
  1.5 0.1 reshape.23
  1.7 0.2 broadcast_in_dim_reshape.3
  1.8 0.4 convert_reduce_fusion
  2.2 0.6 reduce_max.9
  4.1 186.5 %conditional.1 = (f32[4,3,8,128]{3,2,1,0:T(8,128)S(1)}, bf16[64,6144]{1,0:T(8,128)(2,1)S(1)}, bf16[64,6144]{1,0:T(8,128)(2,1)S(1)}, bf16[64,6144]{1,0:T(8,128)(2,1)S(1)}, bf16[64,6144]{1,0:T(8,128)(2,1)S(1)}) conditional(s32[]{:T(128)} %clamp.3, (bf16[64,6144]{1,0:T(8,128)(2,1)}, bf16[64,6144]{1,0:T(8,128)(2,1)}, ...), branch_computations={%region_2.0_spmd.clone.clone, %region_3.0_spmd.clone.clone, %regio... | conditional | bytes 6291496 | solution.py:600
  4.1 183.9 %exchange_160.3 = (bf16[4,64,6144]{2,1,0:T(8,128)(2,1)}, f32[4,3,8,128]{3,2,1,0:T(8,128)S(1)}) custom-call(bf16[64,6144]{1,0:T(8,128)(2,1)} %get-tuple-element.174.query_in, bf16[64,6144]{1,0:T(8,128)(2,1)} %get-tuple-element.175.key_in, bf16[64,6144]{1,0:T(8,128)(2,1)} %get-tuple-element.176.value_in, bf16[512,1536]{1,0:T(8,128)(2,1)} %get-tuple-element.177.grad_in, ...), custom_call_target="tpu_custom_call" | custom-call | tf_op jit(solution)/shard_map/cond/branch_0_fun/exchange_160/pallas_call | solution.py:571
  188.0 2.0 %slice_bitcast_fusion = (bf16[64,6144]{1,0:T(8,128)(2,1)S(1)}, bf16[64,6144]{1,0:T(8,128)(2,1)S(1)}, bf16[64,6144]{1,0:T(8,128)(2,1)S(1)}, bf16[64,6144]{1,0:T(8,128)(2,1)S(1)}) fusion(bf16[4,64,6144]{2,1,0:T(8,128)(2,1)} %get-tuple-element.181), kind=kLoop, calls=%fused_computation | loop fusion | bytes 6291456 | tf_op jit(solution)/shard_map/squeeze | solution.py:605
  190.6 0.0 copy-start
  190.6 0.0 copy-start.1
  190.6 0.0 copy-start.2
  190.7 0.0 copy-start.3
  190.7 0.1 constant_dynamic-slice_fusion.1
  190.8 0.1 copy.23
  190.9 0.9 reshape_squeeze.6
  191.8 0.1 copy.24
  191.9 0.6 reshape_squeeze.7
  192.5 0.0 copy-done
  192.5 0.0 copy-done.1
  192.5 0.0 copy-done.2
  192.5 0.0 copy-done.3
  (2 shorter events, 0.0 us)
Async XLA Ops:
  190.6 1.9 copy-start
  190.6 1.9 copy-start.1
  190.6 1.9 copy-start.2
  190.7 1.9 copy-start.3
